TPU v7x, 128 devices: a whole 4x4x4 slice. The times are simulated.
128 devices in a mesh: tm: 128 (over z, y, x, core).
Axes of the slice: x: 4, y: 4, z: 4, core: 2. Of those that a mesh axis runs over, the one named last changes fastest.
Arguments:
- hidden: bfloat16 [49152, 8192], P('tm'), may hold values from -6 to 6
- norm_gain: float32 [8192], replicated, may hold values from 0.1 to 1.9
- w_in: bfloat16 [8192, 768], replicated, may hold values from -0.0625 to 0.0625
- w_short: float32 [768, 7], replicated, may hold values from -2 to 2
- residues: float32 [8, 16], replicated, may hold values from -4 to 4
- rates: float32 [8, 16], replicated, may hold values from 4.06901042e-06 to 0.0333333333, as said below
- skip: float32 [256], replicated, may hold values from -4 to 4
- w_out: bfloat16 [256, 8192], replicated, may hold values from -0.375 to 0.375
Outputs:
- mixed: bfloat16 [49152, 8192], P('tm')
Inputs may be any that keep to these rules, and one draw needn't show every extreme that they name: `rates`: every rate is positive.
All inputs are finite; a program needn't handle non-finite values.
Results may differ from a plain program's by a relative error of at most 0.0088.
Values may be sent and summed in bfloat16 or wider, within the bound.
No kernel may reach another device: no remote copies, remote signals or barrier semaphores. Data moves between devices by JAX's collectives and lax.ppermute only.
A program may use at most 256 MiB of HBM per device.

v0:
```python
import jax
import jax.numpy as jnp
from jax import lax
from jax.sharding import PartitionSpec as P

HIGHEST = lax.Precision.HIGHEST


def shifted(block, axis, distance):
    devices = range(lax.axis_size(axis))
    route = [(i - distance, i) for i in devices if i - distance in devices]
    return lax.ppermute(block, axis, route)


def own_block(fragment, tok_rows, rates, residues):
    weights = residues * jnp.sqrt(2.0 * rates)
    steps_idx = jnp.arange(tok_rows, dtype=jnp.int32)
    lag_matrix = (steps_idx[None, :] - steps_idx[:, None]).astype(jnp.float32)
    decays = jnp.exp(-rates[:, :, None, None] * jnp.maximum(lag_matrix, 0.0)[None, None, :, :])
    toeplitz = jnp.einsum("gm,gmst->gst", weights, decays, precision=HIGHEST)
    toeplitz = jnp.where((lag_matrix >= 0.0)[None, :, :], toeplitz, 0.0)
    return jnp.einsum(
        "gcs,gst->gct", fragment, toeplitz, precision=HIGHEST, preferred_element_type=jnp.float32
    )


def on_device(hidden, norm_gain, w_in, w_short, residues, rates, skip, w_out):
    tok_rows = hidden.shape[0]
    chan_total = w_short.shape[0] // 3
    group_count = rates.shape[0]
    chan_group = chan_total // group_count
    tap_count = w_short.shape[1]
    own_start = lax.axis_index("tm") * tok_rows
    widened = hidden.astype(jnp.float32)
    inv_scale = lax.rsqrt(jnp.mean(widened * widened, axis=1, keepdims=True) + 1e-06)
    normed = (widened * inv_scale * norm_gain).astype(jnp.bfloat16)
    projected = lax.dot_general(
        w_in, normed, (((0,), (1,)), ((), ())), preferred_element_type=jnp.float32
    ).astype(jnp.bfloat16)
    edge_cols = shifted(projected[:, tok_rows - (tap_count - 1) :], "tm", 1)
    extended = jnp.concatenate([edge_cols, projected], axis=1).astype(jnp.float32)
    features = jnp.zeros(projected.shape, jnp.float32)
    for offset_tap in range(tap_count):
        begin = tap_count - 1 - offset_tap
        features = (
            features
            + w_short[:, offset_tap : offset_tap + 1] * extended[:, begin : begin + tok_rows]
        )
    queries = features[:chan_total]
    keyed = features[chan_total : 2 * chan_total]
    valued = features[2 * chan_total :]
    product = (keyed * valued).astype(jnp.bfloat16)
    product_wide = product.astype(jnp.float32).reshape(group_count, chan_group, tok_rows)
    local_part = own_block(product_wide, tok_rows, rates, residues)
    positions = jnp.arange(tok_rows, dtype=jnp.float32)
    fragment = lax.all_gather(product, "tm", axis=1, tiled=True)
    width = fragment.shape[1]
    spots = jnp.arange(width, dtype=jnp.int32)
    distance = (own_start - 1 - spots).astype(jnp.float32)
    factor = jnp.exp(-rates[:, None, :] * jnp.maximum(distance, 0.0)[None, :, None])
    factor = jnp.where((spots < own_start)[None, :, None], factor, 0.0)
    grouped = fragment.astype(jnp.float32).reshape(group_count, chan_group, width)
    states = jnp.einsum(
        "gcw,gwm->gcm", grouped, factor, precision=HIGHEST, preferred_element_type=jnp.float32
    )
    weights = residues * jnp.sqrt(2.0 * rates)
    rising = jnp.exp(-rates[:, :, None] * (positions + 1.0)[None, None, :])
    convolved = local_part + jnp.einsum(
        "gcm,gmt->gct",
        states * weights[:, None, :],
        rising,
        precision=HIGHEST,
        preferred_element_type=jnp.float32,
    )
    convolved = convolved.reshape(chan_total, tok_rows)
    product_flat = product_wide.reshape(chan_total, tok_rows)
    gated = (queries * (convolved + skip[:, None] * product_flat)).astype(jnp.bfloat16)
    mixed = lax.dot_general(
        gated, w_out, (((0,), (0,)), ((), ())), preferred_element_type=jnp.float32
    )
    return mixed.astype(jnp.bfloat16)


def solution(mesh):
    return jax.shard_map(
        on_device,
        mesh=mesh,
        in_specs=(P("tm", None), P(), P(), P(), P(), P(), P(), P()),
        out_specs=P("tm", None),
        check_vma=False,
    )
```

profile of v0, /device:TPU:32, one launch (start us, length us, event | category | flops | bytes accessed | tf_op | source)
XLA Modules:
  0.0 230.6 jit_solution(6560298311716021537)
XLA Ops:
  6.5 0.0 all-gather.2.cloned.1.call-start
  6.5 0.0 copy-start
  6.5 4.3 %fusion.6 = f32[384]{0:T(512)S(1)} fusion(bf16[384,8192]{1,0:T(8,128)(2,1)} %param.8), kind=kLoop, calls=%fused_computation.9 | loop fusion | flops 9436800 | bytes 6292992 | tf_op jit(solution)/shard_map/reduce_sum | solution.py:35
  10.8 0.3 copy-done
  11.1 0.0 copy-start.2
  11.1 8.3 %fusion.24 = bf16[768,384]{0,1:T(8,128)(2,1)S(1)} fusion(bf16[8192,768]{1,0:T(8,128)(2,1)} %param.10, bf16[384,8192]{1,0:T(8,128)(2,1)S(1)} %copy-done, f32[8192]{0:T(1024)} %param.9, f32[384]{0:T(512)S(1)} %add_rsqrt_fusion), kind=kOutput, calls=%fused_computation.26 | convolution fusion | flops 4844716032 | bytes 19498496 | tf_op jit(solution)/shard_map/dot_general | solution.py:37
  19.5 1.9 collective-permute-start
  21.4 0.0 copy-done.2
  21.4 0.1 slice_reduce_fusion.6
  21.5 7.2 %collective-permute-done = bf16[768,6]{0,1:T(8,128)(2,1)S(1)} collective-permute-done((bf16[768,6]{0,1:T(8,128)(2,1)S(1)}, bf16[768,6]{0,1:T(8,128)(2,1)S(1)}, u32[]{:S(2)}, u32[]{:S(2)}) %collective-permute-start) | collective-permute-done | bytes 9248 | tf_op jit(solution)/shard_map/ppermute | solution.py:12
  28.7 0.1 maximum_convert_fusion
  28.8 0.0 copy-start.4
  28.8 0.0 copy-start.5
  28.9 1.0 fusion.27
  29.8 0.7 fusion.36
  30.5 0.0 all-gather.2.cloned.1.call-update
  30.6 0.1 convert_compare_fusion
  30.7 0.1 convert_maximum_fusion
  30.8 0.0 copy-done.4
  30.8 0.0 copy-done.5
  30.9 24.4 %multiply_exponential_fusion = f32[8,16,384,384]{3,2,1,0:T(8,128)} fusion(f32[384,384]{1,0:T(8,128)S(1)} %convert_maximum_fusion, f32[8,16]{1,0:T(8,128)S(1)} %get-tuple-element.12), kind=kLoop, calls=%fused_computation.2 | loop fusion | flops 18874368 | bytes 76087808 | tf_op jit(solution)/shard_map/exp | solution.py:19
  55.3 0.0 copy-start.1
  55.3 98.0 %fusion = f32[8,1,384,384]{3,1,2,0:T(1,128)} fusion(f32[8,16,1,1]{1,2,3,0:T(1,128)S(1)} %bitcast.20, f32[8,16,384,384]{3,2,1,0:T(8,128)} %multiply_exponential_fusion), kind=kOutput, calls=%fused_computation | convolution fusion | flops 226492416 | bytes 80216576 | tf_op jit(solution)/shard_map/gm,gmst->gst/dot_general | solution.py:20
  153.4 0.0 copy-done.1
  153.4 0.2 copy.14
  153.5 4.4 %fusion.17 = f32[8,32,384]{2,1,0:T(8,128)S(1)} fusion(bf16[8,32,384]{2,1,0:T(8,128)(2,1)S(1)} %bitcast.19, f32[8,1,384,384]{3,1,2,0:T(1,128)} %fusion, pred[384,384]{1,0:T(8,128)(4,1)S(1)} %convert_compare_fusion), kind=kOutput, calls=%fused_computation.21 | convolution fusion | flops 454164480 | bytes 5455872 | tf_op jit(solution)/shard_map/gcs,gst->gct/dot_general | solution.py:22
  157.9 0.0 all-gather.2.cloned.1.call-done
  157.9 32.7 %copy.15 = bf16[256,49152]{1,0:T(8,128)(2,1)} copy(bf16[256,49152]{0,1:T(8,128)(2,1)} %all-gather.2.cloned.1.call-done) | data formatting | bytes 50331648 | tf_op jit(solution)/shard_map/all_gather | solution.py:56
  190.6 0.0 copy-start.3
  190.6 25.6 %fusion.33 = f32[8,32,16]{1,2,0:T(8,128)S(1)} fusion(bf16[8,32,49152]{2,1,0:T(8,128)(2,1)} %bitcast.17, f32[49152]{0:T(1024)S(1)} %convert_maximum_fusion.1, f32[8,16]{1,0:T(8,128)S(1)} %get-tuple-element.12, pred[49152]{0:T(1024)(128)(4,1)S(1)} %iota_compare_fusion, f32[8,16]{1,0:T(8,128)S(1)} %get-tuple-element.13), kind=kOutput, calls=%fused_computation.41 | convolution fusion | flops 2428506112 | bytes 25428992 | tf_op jit(solution)/shard_map/gcw,gwm->gcm/dot_general | solution.py:63
  216.3 0.6 convolution_add_fusion
  216.9 0.2 copy.16
  217.0 0.0 copy-done.3
  217.1 6.7 %convolution_convert_fusion = bf16[384,8192]{1,0:T(8,128)(2,1)} fusion(bf16[256,8192]{1,0:T(8,128)(2,1)} %param.15, f32[768,384]{0,1:T(8,128)S(1)} %fusion.27, f32[256,384]{0,1:T(8,128)S(1)} %copy.16, bf16[256,384]{0,1:T(8,128)(2,1)S(1)} %copy-done.1, f32[256]{0:T(256)S(1)} %copy-done.3), kind=kOutput, calls=%fused_computation.16 | convolution fusion | flops 1614249984 | bytes 11469824 | tf_op jit(solution)/shard_map/dot_general | solution.py:78
  (6 shorter events, 0.1 us)
Async XLA Ops:
  6.5 151.4 %all-gather.2.cloned.1.call-start = ((), (), s32[]{:S(2)}) async-start(), calls=%async_computation | async-start | bytes 25362432 | tf_op jit(solution)/shard_map/all_gather | solution.py:56
  6.5 4.6 %copy-start = (bf16[384,8192]{1,0:T(8,128)(2,1)S(1)}, bf16[384,8192]{1,0:T(8,128)(2,1)}, u32[]{:S(2)}) copy-start(bf16[384,8192]{1,0:T(8,128)(2,1)} %param.8) | copy-start | bytes 18874372
  11.1 10.3 %copy-start.2 = (f32[768,7]{0,1:T(8,128)S(1)}, f32[768,7]{0,1:T(8,128)}, u32[]{:S(2)}) copy-start(f32[768,7]{0,1:T(8,128)} %param.11) | copy-start | bytes 64516
  19.5 9.2 %collective-permute-start = (bf16[768,6]{0,1:T(8,128)(2,1)S(1)}, bf16[768,6]{0,1:T(8,128)(2,1)S(1)}, u32[]{:S(2)}, u32[]{:S(2)}) collective-permute-start(bf16[768,6]{0,1:T(8,128)(2,1)S(1)} %slice.72), channel_id=1, source_target_pairs={{0,1},{1,2},{2,3},{3,4},{4,5},{5,6},{6,7},{7,8},{8,9},{9,10},{10,1... | collective-permute-start | bytes 27656 | tf_op jit(solution)/shard_map/ppermute | solution.py:12
  28.8 2.0 copy-start.4
  28.8 2.0 copy-start.5
  55.3 98.0 %copy-start.1 = (bf16[256,384]{0,1:T(8,128)(2,1)S(1)}, bf16[256,384]{0,1:T(8,128)(2,1)}, u32[]{:S(2)}) copy-start(bf16[256,384]{0,1:T(8,128)(2,1)} %fusion.36) | copy-start | bytes 589828
  190.6 26.4 %copy-start.3 = (f32[256]{0:T(256)S(1)}, f32[256]{0:T(256)}, u32[]{:S(2)}) copy-start(f32[256]{0:T(256)} %param.14) | copy-start | bytes 3076
Sparse Core Ops, SparseCore 0:
  30.7 90.2 all-gather.1
where the time goes:
time: 232 us; the launch traced here: 231 us
  matrix products  144 us (62%)
  local copies, waits for them, and re-layouts  33.5 us (14%)
  other arithmetic  30.8 us (13%)
  between operations  13.6 us (6%)
  waiting for transfers between devices  7.26 us (3%)
    dot_general x1, matrix products, own_block(): toeplitz = jnp.einsum('gm,gmst->gst', weights, decays, precision=HIGHEST)  98 us
    all_gather x1, local copies, waits for them, and re-layouts, on_device(): fragment = lax.all_gather(product, 'tm', axis=1, tiled=True)  32.7 us
    dot_general x1, matrix products, on_device(): jnp.einsum('gcw,gwm->gcm', grouped, factor, precision=HIGHEST, preferred_...  25.6 us
    exp x1, other arithmetic, own_block(): jnp.exp(-rates[:, :, None, None] * jnp.maximum(lag_matrix, 0.0)[None, Non...  24.4 us
    dot_general x1, matrix products, on_device(): lax.dot_general(w_in, normed, (((0,), (1,)), ((), ())), preferred_element...  8.31 us
    ppermute x1, waiting for transfers between devices, shifted(): return lax.ppermute(block, axis, route)  7.22 us
    dot_general x1, matrix products, on_device(): lax.dot_general(gated, w_out, (((0,), (0,)), ((), ())), preferred_element...  6.7 us
  transfers between devices with their start and end apart: 2, of which 1 were waited for; matrix products, arithmetic and copies ran while one was open for 55% of the time, Pallas kernels for 0%

commit v1 on v0

--- a/solution.py
+++ b/solution.py
@@ -53,7 +53,17 @@
     product_wide = product.astype(jnp.float32).reshape(group_count, chan_group, tok_rows)
     local_part = own_block(product_wide, tok_rows, rates, residues)
     positions = jnp.arange(tok_rows, dtype=jnp.float32)
-    fragment = lax.all_gather(product, "tm", axis=1, tiled=True)
+
+    def scan_ratios(field_in):
+        step_out = lax.all_to_all(
+            jnp.stack(tuple((field_in for _ in range(lax.axis_size("tm")))), axis=0),
+            axis_name="tm",
+            split_axis=0,
+            concat_axis=0,
+        )
+        return jnp.concatenate(step_out, axis=1)
+
+    fragment = scan_ratios(product)
     width = fragment.shape[1]
     spots = jnp.arange(width, dtype=jnp.int32)
     distance = (own_start - 1 - spots).astype(jnp.float32)

time: 232 us -> 527 us (2.27)
  the two profiles are of different devices: /device:TPU:32 before, /device:TPU:2 now
where the time goes in v1:
time: 527 us; the launch traced here: 526 us
  waiting for transfers between devices  274 us (52%)
  matrix products  141 us (27%)
  local copies, waits for them, and re-layouts  68.2 us (13%)
  other arithmetic  30 us (6%)
  starting transfers between devices  12.9 us (2%)
    all_to_all x1, waiting for transfers between devices, scan_ratios(): lax.all_to_all(jnp.stack(tuple((field_in for _ in range(lax.axis_size('tm...  271 us
    dot_general x1, matrix products, own_block(): toeplitz = jnp.einsum('gm,gmst->gst', weights, decays, precision=HIGHEST)  97.4 us
    reshape x1, local copies, waits for them, and re-layouts, on_device(): fragment.astype(jnp.float32).reshape(group_count, chan_group, width)  31.2 us
    reshape x1, local copies, waits for them, and re-layouts, scan_ratios(): return jnp.concatenate(step_out, axis=1)  27 us
    dot_general x1, matrix products, on_device(): jnp.einsum('gcw,gwm->gcm', grouped, factor, precision=HIGHEST, preferred_...  25.6 us
    exp x1, other arithmetic, own_block(): jnp.exp(-rates[:, :, None, None] * jnp.maximum(lag_matrix, 0.0)[None, Non...  24.4 us
    all_to_all x1, starting transfers between devices, scan_ratios(): lax.all_to_all(jnp.stack(tuple((field_in for _ in range(lax.axis_size('tm...  10.9 us
  transfers between devices with their start and end apart: 2, of which 2 were waited for; matrix products, arithmetic and copies ran while one was open for 24% of the time, Pallas kernels for 0%

profile of v1, /device:TPU:2, one launch (start us, length us, event | category | flops | bytes accessed | tf_op | source)
XLA Modules:
  0.0 525.7 jit_solution(1991268591618131894)
XLA Ops:
  0.0 0.0 copy-start
  0.0 4.3 fusion.6
  4.3 0.3 copy-done
  4.6 0.0 copy-start.1
  4.6 8.3 %fusion.24 = bf16[768,384]{0,1:T(8,128)(2,1)S(1)} fusion(bf16[8192,768]{1,0:T(8,128)(2,1)} %param.10, bf16[384,8192]{1,0:T(8,128)(2,1)S(1)} %copy-done, f32[8192]{0:T(1024)} %param.9, f32[384]{0:T(512)S(1)} %add_rsqrt_fusion), kind=kOutput, calls=%fused_computation.26 | convolution fusion | flops 4844716032 | bytes 19498496 | tf_op jit(solution)/shard_map/dot_general | solution.py:37
  12.9 1.9 collective-permute-start
  14.9 0.0 copy-done.1
  14.9 0.1 slice_reduce_fusion.6
  14.9 3.0 collective-permute-done
  17.9 0.1 maximum_convert_fusion
  18.1 1.0 fusion.27
  19.1 0.2 copy.15
  19.3 9.2 %stack.2 = bf16[128,256,384]{2,1,0:T(8,128)(2,1)} broadcast(bf16[256,384]{1,0:T(8,128)(2,1)S(1)} %copy.15), dimensions={1,2} | broadcast | bytes 25362432 | tf_op jit(solution)/shard_map/stack | solution.py:59
  28.5 0.0 copy-start.3
  28.5 0.0 copy-start.4
  28.5 10.9 %all-to-all-start = ((bf16[128,256,384]{2,1,0:T(8,128)(2,1)}), bf16[128,256,384]{2,1,0:T(8,128)(2,1)}, u32[]{:S(2)}, u32[]{:S(2)}) async-start(bf16[128,256,384]{2,1,0:T(8,128)(2,1)} %stack.2), calls=%async_computation | async-start | bytes 50331648 | tf_op jit(solution)/shard_map/all_to_all | solution.py:58
  39.4 0.1 convert_compare_fusion
  39.6 0.1 convert_maximum_fusion
  39.7 0.0 copy-done.3
  39.7 0.0 copy-done.4
  39.8 24.4 %multiply_exponential_fusion = f32[8,16,384,384]{3,2,1,0:T(8,128)} fusion(f32[384,384]{1,0:T(8,128)S(1)} %convert_maximum_fusion, f32[8,16]{1,0:T(8,128)S(1)} %get-tuple-element.12), kind=kLoop, calls=%fused_computation.2 | loop fusion | flops 18874368 | bytes 76087808 | tf_op jit(solution)/shard_map/exp | solution.py:19
  64.1 97.4 %fusion = f32[8,1,384,384]{3,1,2,0:T(1,128)S(1)} fusion(f32[8,16,1,1]{1,2,3,0:T(1,128)S(1)} %bitcast.19, f32[8,16,384,384]{3,2,1,0:T(8,128)} %multiply_exponential_fusion), kind=kOutput, calls=%fused_computation | convolution fusion | flops 226492416 | bytes 80216576 | tf_op jit(solution)/shard_map/gm,gmst->gst/dot_general | solution.py:20
  161.5 2.1 fusion.17
  163.7 270.7 %all-to-all-done = bf16[128,256,384]{2,1,0:T(8,128)(2,1)} async-done(((bf16[128,256,384]{2,1,0:T(8,128)(2,1)}), bf16[128,256,384]{2,1,0:T(8,128)(2,1)}, u32[]{:S(2)}, u32[]{:S(2)}) %all-to-all-start) | async-done | bytes 25165856 | tf_op jit(solution)/shard_map/all_to_all | solution.py:58
  434.3 27.0 %copy.17 = bf16[256,128,384]{2,1,0:T(8,128)(2,1)} copy(bf16[256,128,384]{2,0,1:T(8,128)(2,1)} %bitcast.5) | data formatting | bytes 50331648 | tf_op jit(solution)/shard_map/reshape | solution.py:64
  461.3 31.2 %reshape.77 = bf16[8,32,49152]{2,1,0:T(8,128)(2,1)} reshape(bf16[256,128,384]{2,1,0:T(8,128)(2,1)} %copy.17) | data formatting | bytes 50331648 | tf_op jit(solution)/shard_map/reshape | solution.py:72
  492.6 0.0 copy-start.2
  492.6 25.6 %fusion.33 = f32[8,32,16]{1,2,0:T(8,128)S(1)} fusion(bf16[8,32,49152]{2,1,0:T(8,128)(2,1)} %reshape.77, f32[49152]{0:T(1024)S(1)} %convert_maximum_fusion.1, f32[8,16]{1,0:T(8,128)S(1)} %get-tuple-element.12, pred[49152]{0:T(1024)(128)(4,1)S(1)} %iota_compare_fusion, f32[8,16]{1,0:T(8,128)S(1)} %get-tuple-element.13), kind=kOutput, calls=%fused_computation.41 | convolution fusion | flops 2428506112 | bytes 25428992 | tf_op jit(solution)/shard_map/gcw,gwm->gcm/dot_general | solution.py:73
  518.2 0.6 convolution_add_fusion
  518.8 0.2 copy.18
  519.0 0.0 copy-done.2
  519.0 6.7 %convolution_convert_fusion = bf16[384,8192]{1,0:T(8,128)(2,1)} fusion(bf16[256,8192]{1,0:T(8,128)(2,1)} %param.15, f32[768,384]{0,1:T(8,128)S(1)} %fusion.27, f32[256,384]{0,1:T(8,128)S(1)} %copy.18, bf16[256,384]{0,1:T(8,128)(2,1)S(1)} %fusion.36, f32[256]{0:T(256)S(1)} %copy-done.2), kind=kOutput, calls=%fused_computation.16 | convolution fusion | flops 1614249984 | bytes 11469824 | tf_op jit(solution)/shard_map/dot_general | solution.py:88
  (7 shorter events, 0.1 us)
Async XLA Ops:
  0.0 4.6 copy-start
  4.6 10.3 %copy-start.1 = (f32[768,7]{0,1:T(8,128)S(1)}, f32[768,7]{0,1:T(8,128)}, u32[]{:S(2)}) copy-start(f32[768,7]{0,1:T(8,128)} %param.11) | copy-start | bytes 64516
  12.9 5.0 collective-permute-start
  28.5 11.2 %copy-start.3 = (f32[8,16]{1,0:T(8,128)S(1)}, f32[8,16]{1,0:T(8,128)}, u32[]{:S(2)}) copy-start(f32[8,16]{1,0:T(8,128)} %param.13) | copy-start | bytes 1540
  28.5 11.2 %copy-start.4 = (f32[8,16]{1,0:T(8,128)S(1)}, f32[8,16]{1,0:T(8,128)}, u32[]{:S(2)}) copy-start(f32[8,16]{1,0:T(8,128)} %param.12) | copy-start | bytes 1540
  28.5 405.8 %all-to-all-start = ((bf16[128,256,384]{2,1,0:T(8,128)(2,1)}), bf16[128,256,384]{2,1,0:T(8,128)(2,1)}, u32[]{:S(2)}, u32[]{:S(2)}) async-start(bf16[128,256,384]{2,1,0:T(8,128)(2,1)} %stack.2), calls=%async_computation | async-start | bytes 50331648 | tf_op jit(solution)/shard_map/all_to_all | solution.py:58
  492.6 26.4 %copy-start.2 = (f32[256]{0:T(256)S(1)}, f32[256]{0:T(256)}, u32[]{:S(2)}) copy-start(f32[256]{0:T(256)} %param.14) | copy-start | bytes 3076
